TPU v7x, 256 devices: a whole 4x4x8 slice. The times are simulated.
256 devices in a mesh: ctx: 32 (over x, z), kv: 8 (over y, core).
Axes of the slice: x: 4, y: 4, z: 8, core: 2. Of those that a mesh axis runs over, the one named last changes fastest.
Arguments:
- ctx_query: bfloat16 [8, 16384, 1024], P('kv', 'ctx'), may hold values from -140 to 140
- ctx_kv: bfloat16 [2, 8, 16384, 128], P(None, 'kv', 'ctx'), may hold values from -6 to 6
- new_query: bfloat16 [8, 256, 1024], P('kv', 'ctx'), may hold values from -140 to 140
- new_kv: bfloat16 [2, 8, 256, 128], P(None, 'kv', 'ctx'), may hold values from -6 to 6
- out_weight: bfloat16 [8192, 8192], P('kv', 'ctx'), may hold values from -0.0625 to 0.0625
Outputs:
- ctx_out: bfloat16 [8, 16384, 1024], P('kv', 'ctx')
- new_out: bfloat16 [256, 8192], P('kv', 'ctx')
All inputs are finite; a program needn't handle non-finite values.
Results may differ from a plain program's by a relative error of at most 0.0045.
Values may be sent and summed in bfloat16 or wider, within the bound.
A program may use at most 192 MiB of HBM per device.

v0:
```python
import jax
import jax.numpy as jnp
from jax import lax
from jax.sharding import PartitionSpec as P

GROUP = 8


def spread(shard, axis, root):
    mine = lax.axis_index(axis) == root
    return lax.psum(jnp.where(mine, shard, jnp.zeros_like(shard)), axis)


def merged_2(value, axis, join):
    pieces = jax.tree.map(lambda part: lax.all_gather(part, axis), value)
    head = jax.tree.map(lambda part: part[0], pieces)
    tail = jax.tree.map(lambda part: part[1:], pieces)
    total, _ = lax.scan(lambda total, section: (join(total, section), None), head, tail)
    return total


def stats(queries, keys, values, visible):
    width = keys.shape[1]
    tops = []
    totals = []
    sums = []
    for head in range(GROUP):
        part = queries[:, head * width : (head + 1) * width]
        scores = jnp.dot(part, keys.T, preferred_element_type=jnp.float32) * width ** (-0.5)
        scores = jnp.where(visible, scores, -1e30)
        top = jnp.max(scores, axis=-1)
        weights = jnp.where(visible, jnp.exp(scores - top[:, None]), 0.0)
        tops.append(top)
        totals.append(jnp.sum(weights, axis=-1))
        sums.append(
            jnp.dot(weights.astype(jnp.bfloat16), values, preferred_element_type=jnp.float32)
        )
    return (jnp.stack(tops), jnp.stack(totals), jnp.stack(sums))


def combine(first, second):
    top = jnp.maximum(first[0], second[0])
    left = jnp.exp(first[0] - top)
    right = jnp.exp(second[0] - top)
    return (
        top,
        first[1] * left + second[1] * right,
        first[2] * left[..., None] + second[2] * right[..., None],
    )


def finish(total, summed):
    rows = total.shape[1]
    return (summed / total[..., None]).transpose(1, 0, 2).reshape(rows, -1).astype(jnp.bfloat16)


def body(ctx_query, ctx_kv, new_query, new_kv, out_weight):
    block = ctx_kv.shape[2]
    fresh = new_kv.shape[2]
    here = lax.axis_index("ctx")
    anchor = spread(ctx_kv, "ctx", 0)
    keys = jnp.concatenate([anchor[0, 0], ctx_kv[0, 0]], 0)
    values = jnp.concatenate([anchor[1, 0], ctx_kv[1, 0]], 0)
    row = lax.broadcasted_iota(jnp.int32, (block, 2 * block), 0)
    col = lax.broadcasted_iota(jnp.int32, (block, 2 * block), 1)
    visible = jnp.where(col < block, here > 0, col - block <= row)
    top, total, summed = stats(ctx_query[0], keys, values, visible)
    ctx_out = finish(total, summed)[None]
    local_cache = jnp.concatenate([ctx_kv, new_kv], 2)
    span = block + fresh
    queries = lax.all_gather(new_query, "ctx", axis=1, tiled=True)[0]
    count = queries.shape[0]
    q_row = lax.broadcasted_iota(jnp.int32, (count, span), 0)
    q_col = lax.broadcasted_iota(jnp.int32, (count, span), 1)
    seen = (q_col < block) | (q_col - block + here * fresh <= q_row)
    partial_value = stats(queries, local_cache[0, 0], local_cache[1, 0], seen)
    merged = merged_2(partial_value, "ctx", combine)
    everyone = finish(merged[1], merged[2])
    new_out = lax.psum_scatter(
        jnp.dot(everyone, out_weight, preferred_element_type=jnp.float32),
        "kv",
        scatter_dimension=0,
        tiled=True,
    ).astype(jnp.bfloat16)
    return (ctx_out, new_out)


def solution(mesh):
    return jax.shard_map(
        body,
        mesh=mesh,
        in_specs=(
            P("kv", "ctx", None),
            P(None, "kv", "ctx", None),
            P("kv", "ctx", None),
            P(None, "kv", "ctx", None),
            P("kv", "ctx"),
        ),
        out_specs=(P("kv", "ctx", None), P("kv", "ctx")),
        check_vma=False,
    )
```

profile of v0, /device:TPU:1, one launch (start us, length us, event | category | flops | bytes accessed | tf_op | source)
XLA Modules:
  0.0 541.7 jit_solution(13101501132317487889)
XLA Ops:
  7.2 1.8 constant_dynamic-update-slice_fusion.1
  9.1 42.6 %all_gather.21 = bf16[1,256,1024]{2,1,0:T(8,128)(2,1)S(1)} all-gather(bf16[1,8,1024]{2,1,0:T(8,128)(2,1)} %param.9), channel_id=1, replica_groups=mesh['ctx'=32,'kv'=8] {'ctx'}, dimensions={1}, use_global_device_ids=true | all-gather | bytes 540672 | tf_op jit(solution)/shard_map/all_gather | solution.py:71
  58.5 0.8 copy-done.21
  59.8 1.0 copy-done.13
  60.9 2.6 fusion.108
  63.5 36.7 %all-gather.1 = f32[256,256]{1,0:T(8,128)S(1)} all-gather(f32[8,256]{1,0:T(8,128)S(1)} %stack.170), channel_id=3, replica_groups=mesh['ctx'=32,'kv'=8] {'ctx'}, dimensions={0}, use_global_device_ids=true | all-gather | bytes 270336 | tf_op jit(solution)/shard_map/all_gather | solution.py:15
  100.3 35.3 %all-gather = f32[256,256]{1,0:T(8,128)S(1)} all-gather(f32[8,256]{1,0:T(8,128)S(1)} %stack.161), channel_id=2, replica_groups=mesh['ctx'=32,'kv'=8] {'ctx'}, dimensions={0}, use_global_device_ids=true | all-gather | bytes 270336 | tf_op jit(solution)/shard_map/all_gather | solution.py:15
  135.7 0.7 slice_bitcast_fusion.1
  136.4 18.4 %all-reduce.2.cloned.1.call-done = bf16[2,1,512,128]{3,2,1,0:T(8,128)(2,1)} async-done(((bf16[2,1,512,128]{3,2,1,0:T(8,128)(2,1)}), bf16[2,1,512,128]{3,2,1,0:T(8,128)(2,1)}) %all-reduce.2.cloned.1.call-update) | async-done | bytes 262160 | tf_op jit(solution)/shard_map/psum | solution.py:11
  154.8 1.6 slice_bitcast_fusion.4
  159.9 2.1 fusion.188
  162.0 1.6 fusion.189
  163.7 1.8 fusion.182
  165.5 4.3 fusion.18
  169.9 4.0 fusion.43
  173.9 1.6 fusion.42
  175.7 1.6 fusion.41
  177.3 1.6 fusion.40
  178.9 1.6 fusion.39
  180.5 1.6 fusion.38
  182.1 1.6 fusion.37
  183.6 208.6 %all-gather.5.cloned.1.call-done = f32[256,256,128]{2,1,0:T(8,128)} async-done(((f32[8,256,128]{2,1,0:T(8,128)}), f32[256,256,128]{2,1,0:T(8,128)}) %all-gather.5.cloned.1.call-update) | async-done | bytes 33554448 | tf_op jit(solution)/shard_map/all_gather | solution.py:15
  392.3 22.8 %slice.143 = f32[248,256,128]{2,1,0:T(8,128)} slice(f32[256,256,128]{2,1,0:T(8,128)} %all-gather.5.cloned.1.call-done), slice={[8:256], [0:256], [0:128]} | slice | bytes 65011712 | tf_op jit(solution)/shard_map/slice | solution.py:17
  415.1 88.8 %while.14 = (s32[]{:T(128)}, f32[8,256]{1,0:T(8,128)S(1)}, f32[8,256]{1,0:T(8,128)S(1)}, f32[8,256,128]{2,1,0:T(8,128)S(1)}, f32[31,8,256]{2,1,0:T(8,128)}, /*in...) while((s32[]{:T(128)}, f32[8,256]{1,0:T(8,128)S(1)}, f32[8,256]{1,0:T(8,128)S(1)}, ...), condition=%wide.region_34.35_spmd, body=%wide.region_33.34_spmd.sunk | while | flops 798722 | bytes 3227749 | solution.py:18
  415.1 0.7 fusion.203
  415.8 2.1 fusion.204
  418.0 0.7 fusion.203
  418.7 2.1 fusion.204
  420.8 0.7 fusion.203
  421.5 2.1 fusion.204
  424.4 2.1 fusion.204
  427.3 2.1 fusion.204
  430.1 2.1 fusion.204
  433.0 2.1 fusion.204
  435.9 2.1 fusion.204
  438.7 2.1 fusion.204
  441.6 2.1 fusion.204
  444.4 2.1 fusion.204
  447.3 2.1 fusion.204
  450.2 2.1 fusion.204
  453.0 2.1 fusion.204
  455.9 2.1 fusion.204
  458.8 2.1 fusion.204
  461.6 2.1 fusion.204
  464.5 2.1 fusion.204
  467.4 2.1 fusion.204
  470.2 2.1 fusion.204
  473.1 2.1 fusion.204
  475.9 2.1 fusion.204
  478.8 2.1 fusion.204
  481.7 2.1 fusion.204
  484.5 2.1 fusion.204
  487.4 2.1 fusion.204
  490.3 2.1 fusion.204
  493.1 2.1 fusion.204
  496.0 2.1 fusion.204
  498.9 2.1 fusion.204
  501.7 2.1 fusion.204
  504.3 1.0 fusion.198
  505.4 3.9 fusion.36
  509.3 1.9 divide_convert_fusion
  511.2 1.3 copy.11
  512.5 21.3 %reduce-scatter.2.cloned.1.call-done = f32[32,256]{1,0:T(8,128)} async-done(((f32[256,256]{1,0:T(8,128)}), f32[32,256]{1,0:T(8,128)}) %reduce-scatter.2.cloned.1.call-update) | async-done | bytes 32784 | tf_op jit(solution)/shard_map/reduce_scatter | solution.py:79
  533.8 1.4 convert_element_type.98
  (123 shorter events, 31.5 us)
Async XLA Ops:
  7.2 497.2 %copy-start = (bf16[1024,256]{1,0:T(8,128)(2,1)S(1)}, bf16[1024,256]{1,0:T(8,128)(2,1)}, u32[]{:S(2)}) copy-start(bf16[1024,256]{1,0:T(8,128)(2,1)} %param.11) | copy-start | bytes 1572868
  7.2 147.6 %all-reduce.2.cloned.1.call-start = ((), (), s32[]{:S(2)}) async-start(), calls=%async_computation.1 | async-start | bytes 524288 | tf_op jit(solution)/shard_map/psum | solution.py:11
  9.0 383.2 %all-gather.5.cloned.1.call-start = ((), (), s32[]{:S(2)}) async-start(), calls=%async_computation.3 | async-start | bytes 34603008 | tf_op jit(solution)/shard_map/all_gather | solution.py:15
  53.8 2.9 copy-start.17
  54.2 3.1 copy-start.18
  54.5 3.2 copy-start.19
  54.9 1.9 copy-start.20
  58.5 0.8 copy-start.21
  59.8 1.0 copy-start.13
  60.8 473.0 %reduce-scatter.2.cloned.1.call-start = ((), (), s32[]{:S(2)}) async-start(), calls=%async_computation.2 | async-start | bytes 294912 | tf_op jit(solution)/shard_map/reduce_scatter | solution.py:79
  60.9 74.7 %copy-start.16 = (bf16[2,1,512,128]{3,2,1,0:T(8,128)(2,1)S(1)}, bf16[2,1,512,128]{3,2,1,0:T(8,128)(2,1)}, u32[]{:S(2)}) copy-start(bf16[2,1,512,128]{3,2,1,0:T(8,128)(2,1)} %param.8) | copy-start | bytes 786436
  63.5 92.9 %copy-start.25 = (bf16[1,512,1024]{2,1,0:T(8,128)(2,1)S(1)}, bf16[1,512,1024]{2,1,0:T(8,128)(2,1)}, u32[]{:S(2)}) copy-start(bf16[1,512,1024]{2,1,0:T(8,128)(2,1)} %param.7) | copy-start | bytes 3145732
  100.2 56.8 %copy-start.14 = (f32[256,256]{1,0:T(8,128)}, f32[256,256]{1,0:T(8,128)S(1)}, u32[]{:S(2)}) copy-start(f32[256,256]{1,0:T(8,128)S(1)} %all-gather.1) | copy-start | bytes 786436
  135.6 21.5 %copy-start.15 = (f32[256,256]{1,0:T(8,128)}, f32[256,256]{1,0:T(8,128)S(1)}, u32[]{:S(2)}) copy-start(f32[256,256]{1,0:T(8,128)S(1)} %all-gather) | copy-start | bytes 786436
  135.6 23.6 %copy-start.23 = (bf16[512,128]{1,0:T(8,128)(2,1)}, bf16[512,128]{1,0:T(8,128)(2,1)S(1)}, u32[]{:S(2)}) copy-start(bf16[512,128]{1,0:T(8,128)(2,1)S(1)} %get-tuple-element.87) | copy-start | bytes 393220
  157.1 8.3 %copy-start.10 = (f32[512,1024]{0,1:T(8,128)}, f32[512,1024]{0,1:T(8,128)S(1)}, u32[]{:S(2)}) copy-start(f32[512,1024]{0,1:T(8,128)S(1)} %get-tuple-element.91) | copy-start | bytes 6291460
  157.8 7.6 %copy-start.8 = (f32[512,1024]{0,1:T(8,128)}, f32[512,1024]{0,1:T(8,128)S(1)}, u32[]{:S(2)}) copy-start(f32[512,1024]{0,1:T(8,128)S(1)} %get-tuple-element.93) | copy-start | bytes 6291460
  158.5 6.9 %copy-start.6 = (f32[512,1024]{0,1:T(8,128)}, f32[512,1024]{0,1:T(8,128)S(1)}, u32[]{:S(2)}) copy-start(f32[512,1024]{0,1:T(8,128)S(1)} %get-tuple-element.95) | copy-start | bytes 6291460
  159.2 6.2 %copy-start.4 = (f32[512,1024]{0,1:T(8,128)}, f32[512,1024]{0,1:T(8,128)S(1)}, u32[]{:S(2)}) copy-start(f32[512,1024]{0,1:T(8,128)S(1)} %get-tuple-element.97) | copy-start | bytes 6291460
  159.9 5.6 %copy-start.2 = (f32[512,1024]{0,1:T(8,128)}, f32[512,1024]{0,1:T(8,128)S(1)}, u32[]{:S(2)}) copy-start(f32[512,1024]{0,1:T(8,128)S(1)} %get-tuple-element.99) | copy-start | bytes 6291460
  159.9 2.1 copy-start.24
  163.6 6.2 %copy-start.1 = (f32[512,1024]{0,1:T(8,128)}, f32[512,1024]{0,1:T(8,128)S(1)}, u32[]{:S(2)}) copy-start(f32[512,1024]{0,1:T(8,128)S(1)} %get-tuple-element.103) | copy-start | bytes 6291460
  165.4 4.4 copy-start.12
  165.5 4.4 copy-start.22
  169.9 4.1 copy-start.11
  173.9 1.7 copy-start.9
  175.7 1.6 copy-start.7
  177.3 1.6 copy-start.5
  178.9 1.6 copy-start.3
  392.3 22.8 %slice-start = ((f32[256,256,128]{2,1,0:T(8,128)}), f32[8,256,128]{2,1,0:T(8,128)S(1)}, s32[]{:S(2)}) async-start(f32[256,256,128]{2,1,0:T(8,128)} %all-gather.5.cloned.1.call-done), calls=%async_computation.4 | async-start | bytes 2097152 | tf_op jit(solution)/shard_map/slice | solution.py:16
  392.3 22.8 %slice-start.1 = ((f32[256,256]{1,0:T(8,128)}), f32[8,256]{1,0:T(8,128)S(1)}, s32[]{:S(2)}) async-start(f32[256,256]{1,0:T(8,128)} %copy-done.14), calls=%async_computation.5 | async-start | bytes 16384 | tf_op jit(solution)/shard_map/slice | solution.py:16
  392.3 22.8 %slice-start.2 = ((f32[256,256]{1,0:T(8,128)}), f32[8,256]{1,0:T(8,128)S(1)}, s32[]{:S(2)}) async-start(f32[256,256]{1,0:T(8,128)} %copy-done.15), calls=%async_computation.6 | async-start | bytes 16384 | tf_op jit(solution)/shard_map/slice | solution.py:16
Sparse Core Ops, SparseCore 0:
  11.5 143.2 all-reduce.1
  157.9 234.2 all-gather.4
  505.5 28.2 reduce-scatter.1
where the time goes:
time: 546 us; the launch traced here: 542 us
  waiting for transfers between devices  248 us (45%)
  blocking collectives  115 us (21%)
  other arithmetic  100 us (18%)
  matrix products  33.8 us (6%)
  local copies, waits for them, and re-layouts  29.7 us (5%)
  between operations  14.2 us (3%)
    all_gather x1, waiting for transfers between devices, merged_2(): pieces = jax.tree.map(lambda part: lax.all_gather(part, axis), value)  209 us
    all_gather x2, blocking collectives, merged_2(): pieces = jax.tree.map(lambda part: lax.all_gather(part, axis), value)  72 us
    add x31, other arithmetic, combine(): first[2] * left[..., None] + second[2] * right[..., None]  66 us
    all_gather x1, blocking collectives, body(): queries = lax.all_gather(new_query, 'ctx', axis=1, tiled=True)[0]  42.6 us
    slice x3, local copies, waits for them, and re-layouts, merged_2(): tail = jax.tree.map(lambda part: part[1:], pieces)  23.6 us
    add x31, other arithmetic, combine(): first[1] * left + second[1] * right  22.1 us
    reduce_scatter x1, waiting for transfers between devices, body(): lax.psum_scatter(jnp.dot(everyone, out_weight, preferred_element_type=jnp...  21.3 us
    dot_general x16, matrix products, stats(): jnp.dot(weights.astype(jnp.bfloat16), values, preferred_element_type=jnp....  21.2 us
  transfers between devices with their start and end apart: 3, of which 3 were waited for; matrix products, arithmetic and copies ran while one was open for 9% of the time, Pallas kernels for 0%

commit v1 on v0

v1 whole, which is shorter than its diff:
```python
import math

import jax
import jax.numpy as jnp
from jax import lax
from jax.experimental import pallas as pl
from jax.experimental.pallas import tpu as pltpu
from jax.sharding import PartitionSpec as P

HD = 128
GROUP = 8
BLK = 512
NX, NZ, NY, NC = 4, 8, 4, 2
NCTX, NKV = NX * NZ, NY * NC
QT = 8
ROWS = QT * GROUP
PIECE = BLK // NZ
SCALE = HD**-0.5 * math.log2(math.e)
LOW = -1e30
ZS = (1, 7, 2, 6, 3, 5, 4)
XS = (1, 3, 2)
KVS = ((0, 1), (1, 0), (3, 0), (1, 1), (3, 1), (2, 0), (2, 1))
F32, BF16 = jnp.float32, jnp.bfloat16


def rcopy(src, dst, send, recv, dev):
    return pltpu.make_async_remote_copy(
        src_ref=src,
        dst_ref=dst,
        send_sem=send,
        recv_sem=recv,
        device_id=dev,
        device_id_type=pl.DeviceIdType.MESH,
    )


def scores(q, k):
    return lax.dot_general(q, k, (((1,), (1,)), ((), ())), preferred_element_type=F32) * SCALE


def with_ones(v):
    return jnp.concatenate([v, jnp.ones_like(v)], axis=1)


def weigh(s, top, v1):
    return jnp.dot(jnp.exp2(s - top).astype(BF16), v1, preferred_element_type=F32)


def kernel(
    cq_h, ckv_h, nq_ref, nkv_ref, w_h,
    co_h, no_ref,
    cq, kv, w, fresh, qbuf, anc, own_n, own_m, out, q_n, q_m,
    n_send, n_recv, st_send, st_recv, att, po, po_recv,
    loc, q_ss, q_rs, kv_ss, kv_rs, n_ss, n_rs, an_ss, an_rs, sc_ss, sc_rs,
    az_ss, az_rs, ax_ss, ax_rs, po_ss, po_rs,
):
    here = lax.axis_index("ctx")
    head = lax.axis_index("kv")
    x, z, y, co = here // NZ, here % NZ, head // NC, head % NC

    def zdev(d):
        return (x * NZ + (z + d) % NZ, head)

    def xdev(e):
        return ((x + e) % NX * NZ + z, head)

    def kvdev(dy, dc):
        return (here, (y + dy) % NY * NC + (co + dc) % NC)

    barrier = pltpu.get_barrier_semaphore()
    peers = [zdev(d) for d in ZS] + [xdev(e) for e in XS] + [kvdev(*k) for k in KVS]
    for dev in peers:
        pl.semaphore_signal(barrier, inc=1, device_id=dev, device_id_type=pl.DeviceIdType.MESH)
    load_kv = pltpu.make_async_copy(ckv_h.at[:, 0], kv.at[0], loc.at[0])
    load_cq = pltpu.make_async_copy(cq_h.at[0], cq, loc.at[1])
    load_w = pltpu.make_async_copy(w_h, w, loc.at[2])
    load_kv.start()
    load_cq.start()
    load_w.start()
    nq = nq_ref[0].astype(F32)
    qbuf[0] = jnp.concatenate([nq[:, g * HD : (g + 1) * HD] for g in range(GROUP)], 0).astype(BF16)
    nkv = nkv_ref[:, 0].astype(F32)
    fresh[0] = jnp.concatenate([nkv, jnp.zeros_like(nkv)], 1).astype(BF16)
    pl.semaphore_wait(barrier, len(peers))

    q_copies = {d: rcopy(qbuf.at[0], qbuf.at[d], q_ss.at[d], q_rs.at[d], zdev(d)) for d in ZS}
    for d in ZS:
        q_copies[d].start()
    kv_copies = {}
    for part in range(2):
        for e in XS:
            kv_copies[e, part] = rcopy(
                ckv_h.at[part, 0], kv.at[e, part], kv_ss.at[part, e], kv_rs.at[part, e], xdev(e)
            )
            kv_copies[e, part].start()
        if part == 0:
            for e in XS:
                kv_copies[e, 2] = rcopy(
                    fresh.at[0], fresh.at[e], kv_ss.at[2, e], kv_rs.at[2, e], xdev(e)
                )
                kv_copies[e, 2].start()

    load_kv.wait()
    load_cq.wait()

    def own_head(g, carry):
        cols = pl.ds(pl.multiple_of(g * HD, HD), HD)
        for r in range(4):
            width = (r + 1) * 128
            q = cq[pl.ds(r * 128, 128), cols]
            s = scores(q, kv[0, 0, pl.ds(0, width), :])
            row = lax.broadcasted_iota(jnp.int32, (128, width), 0) + r * 128
            col = lax.broadcasted_iota(jnp.int32, (128, width), 1)
            s = jnp.where(col <= row, s, LOW)
            top = jnp.max(s, axis=1, keepdims=True)
            own_n[g, pl.ds(r * 128, 128), :] = weigh(s, top, with_ones(kv[0, 1, pl.ds(0, width), :]))
            own_m[g, pl.ds(r * 128, 128), :] = jnp.broadcast_to(top, (128, HD))
        return carry

    lax.fori_loop(0, GROUP, own_head, 0)

    for d in ZS:
        q_copies[d].wait_recv()

    def query_block(e):
        def rows(c, carry):
            at = pl.ds(pl.multiple_of(c * 128, 128), 128)
            q = qbuf[pl.ds(c * 2, 2)].reshape(128, HD)
            s = scores(q, kv[e, 0])
            top = jnp.max(s, axis=1, keepdims=True)
            if e == 0:
                q_n[at, :] = weigh(s, top, with_ones(kv[e, 1]))
            else:
                old = q_m[at, :][:, :1]
                top = jnp.maximum(top, old)
                q_n[at, :] = q_n[at, :] * jnp.exp2(old - top) + weigh(s, top, with_ones(kv[e, 1]))
            q_m[at, :] = jnp.broadcast_to(top, (128, HD))
            return carry

        lax.fori_loop(0, NZ * ROWS // 128, rows, 0)

    query_block(0)
    for e in XS:
        kv_copies[e, 0].wait_recv()
        kv_copies[e, 1].wait_recv()
        query_block(e)
    for e in XS:
        kv_copies[e, 2].wait_recv()

    q = qbuf[...].reshape(NZ * ROWS, HD)
    s = scores(q, fresh[:, 0].reshape(NX * 16, HD))
    row = lax.broadcasted_iota(jnp.int32, s.shape, 0)
    col = lax.broadcasted_iota(jnp.int32, s.shape, 1)
    token = (x * NZ + (z - row // ROWS + NZ) % NZ) * QT + row % QT
    key = ((x - col // 16 + NX) % NX * NZ + z) * QT + col % 16
    s = jnp.where((col % 16 < QT) & (key <= token), s, LOW)
    old = q_m[...][:, :1]
    top = jnp.maximum(jnp.max(s, axis=1, keepdims=True), old)
    total = q_n[...] * jnp.exp2(old - top) + weigh(s, top, with_ones(fresh[:, 1].reshape(NX * 16, HD)))
    n_send[...] = (total[:, :HD] / total[:, HD:]).astype(BF16).reshape(NZ, ROWS, HD)
    lse = (top + jnp.log2(total[:, HD:])).reshape(NZ, GROUP, QT, HD)
    lane = lax.broadcasted_iota(jnp.int32, (NZ, QT, HD), 2)
    stat = jnp.full((NZ, QT, HD), 0.0, F32)
    for g in range(GROUP):
        stat = jnp.where(lane == g, lse[:, g], stat)
    st_send[...] = stat

    n_copies = []
    for d in ZS:
        n_copies.append(rcopy(st_send.at[d], st_recv.at[d], n_ss.at[0, d], n_rs.at[0, d], zdev(NZ - d)))
        n_copies.append(rcopy(n_send.at[d], n_recv.at[d], n_ss.at[1, d], n_rs.at[1, d], zdev(NZ - d)))
    for c in n_copies:
        c.start()

    def piece(ref, p):
        return ref.at[:, pl.ds(pl.multiple_of(p * PIECE, PIECE), PIECE)]

    local_anchor = pltpu.make_async_copy(kv.at[x], anc, loc.at[3])
    scatters = [rcopy(piece(kv.at[x], p), piece(anc, p), sc_ss.at[p], sc_rs, zdev(p)) for p in range(1, NZ)]

    @pl.when(z == 0)
    def _():
        for c in scatters:
            c.start()
        local_anchor.start()
        local_anchor.wait()

    @pl.when(z > 0)
    def _():
        rcopy(piece(kv.at[0], 0), piece(anc, z), sc_ss.at[0], sc_rs, zdev(1)).wait_recv()

    spreads = {d: rcopy(piece(anc, z), piece(anc, z), an_ss.at[d], an_rs.at[d], zdev(d)) for d in ZS}
    for d in ZS:

        @pl.when((z + d) % NZ != 0)
        def _():
            spreads[d].start()

    for c in n_copies:
        c.wait_recv()
    st_recv[0] = st_send[0]
    n_recv[0] = n_send[0]
    stats = st_recv[...]
    peak = jnp.max(stats, axis=0)
    share = jnp.exp2(stats - peak[None])
    share = share / jnp.sum(share, axis=0)[None]
    parts = n_recv[...].astype(F32)
    pieces = []
    for g in range(GROUP):
        pieces.append(jnp.sum(parts[:, g * QT : (g + 1) * QT] * share[:, :, g : g + 1], axis=0))
    att[here] = jnp.concatenate(pieces, 0).astype(BF16)

    az = {d: rcopy(att.at[here], att.at[here], az_ss.at[d], az_rs.at[d], zdev(d)) for d in ZS}
    for d in ZS:
        az[d].start()
    ax = {}

    def forward(d):
        block = x * NZ + (z - d + NZ) % NZ
        for e in XS:
            ax[d, e] = rcopy(att.at[block], att.at[block], ax_ss.at[d, e], ax_rs.at[d, e], xdev(e))
            ax[d, e].start()

    forward(0)
    for d in ZS:
        az[d].wait_recv()
        forward(d)

    @pl.when(z > 0)
    def _():
        for d in ZS:
            spreads[d].wait_recv()

    def anchor_head(g, carry):
        cols = pl.ds(pl.multiple_of(g * HD, HD), HD)
        for r in range(4):
            at = pl.ds(r * 128, 128)
            s = scores(cq[at, cols], anc[0])
            top = jnp.max(s, axis=1, keepdims=True)
            n = weigh(s, top, with_ones(anc[1]))
            old = own_m[g, at, :]
            peak = jnp.maximum(old, top)
            mine = jnp.where(here > 0, jnp.exp2(old - peak), 1.0)
            theirs = jnp.where(here > 0, jnp.exp2(top - peak), 0.0)
            summed = own_n[g, at, :]
            total = summed[:, HD:] * mine + n[:, HD:] * theirs
            out[at, cols] = ((summed[:, :HD] * mine + n[:, :HD] * theirs) / total).astype(BF16)
        return carry

    lax.fori_loop(0, GROUP, anchor_head, 0)
    store_out = pltpu.make_async_copy(out, co_h.at[0], loc.at[4])
    store_out.start()

    load_w.wait()
    for c in ax.values():
        c.wait_recv()
    acc = jnp.zeros((NCTX * QT, no_ref.shape[1]), F32)
    for j in range(GROUP // 2):
        pair = att[:, pl.ds(j * 16, 16), :].astype(F32)
        lhs = jnp.concatenate(
            [pair[:, :QT].reshape(NCTX * QT, HD), pair[:, QT:].reshape(NCTX * QT, HD)], 1
        ).astype(BF16)
        acc = acc + jnp.dot(lhs, w[pl.ds(j * 256, 256), :], preferred_element_type=F32)
    po[...] = acc.reshape(po.shape)
    po_copies = []
    for i, (dy, dc) in enumerate(KVS):
        dest = (y + dy) % NY * NC + (co + dc) % NC
        po_copies.append(rcopy(po.at[dest], po_recv.at[i], po_ss.at[i], po_rs.at[i], (here, dest)))
        po_copies[i].start()
    total = po[head]
    for i, c in enumerate(po_copies):
        c.wait_recv()
        total = total + po_recv[i]
    no_ref[...] = total.astype(BF16)

    for group in (q_copies, kv_copies, az, ax):
        for c in group.values():
            c.wait_send()
    for c in n_copies + po_copies:
        c.wait_send()
    for d in ZS:

        @pl.when((z + d) % NZ != 0)
        def _():
            spreads[d].wait_send()

    @pl.when(z == 0)
    def _():
        for c in scatters:
            c.wait_send()

    store_out.wait()


def body(ctx_query, ctx_kv, new_query, new_kv, out_weight):
    any_space = pl.BlockSpec(memory_space=pl.ANY)
    vmem = pl.BlockSpec(memory_space=pltpu.VMEM)
    cols = out_weight.shape[1]
    mine = NCTX * QT // NKV
    dma = pltpu.SemaphoreType.DMA
    return pl.pallas_call(
        kernel,
        out_shape=(
            jax.ShapeDtypeStruct(ctx_query.shape, BF16),
            jax.ShapeDtypeStruct((mine, cols), BF16),
        ),
        in_specs=[any_space, any_space, vmem, vmem, any_space],
        out_specs=(any_space, vmem),
        scratch_shapes=[
            pltpu.VMEM((BLK, GROUP * HD), BF16),
            pltpu.VMEM((NX, 2, BLK, HD), BF16),
            pltpu.VMEM((GROUP * HD, cols), BF16),
            pltpu.VMEM((NX, 2, 16, HD), BF16),
            pltpu.VMEM((NZ, ROWS, HD), BF16),
            pltpu.VMEM((2, BLK, HD), BF16),
            pltpu.VMEM((GROUP, BLK, 2 * HD), F32),
            pltpu.VMEM((GROUP, BLK, HD), F32),
            pltpu.VMEM((BLK, GROUP * HD), BF16),
            pltpu.VMEM((NZ * ROWS, 2 * HD), F32),
            pltpu.VMEM((NZ * ROWS, HD), F32),
            pltpu.VMEM((NZ, ROWS, HD), BF16),
            pltpu.VMEM((NZ, ROWS, HD), BF16),
            pltpu.VMEM((NZ, QT, HD), F32),
            pltpu.VMEM((NZ, QT, HD), F32),
            pltpu.VMEM((NCTX, ROWS, HD), BF16),
            pltpu.VMEM((NKV, mine, cols), F32),
            pltpu.VMEM((NKV - 1, mine, cols), F32),
            dma((5,)),
            dma((NZ,)), dma((NZ,)),
            dma((3, NX)), dma((3, NX)),
            dma((2, NZ)), dma((2, NZ)),
            dma((NZ,)), dma((NZ,)),
            dma((NZ,)), dma,
            dma((NZ,)), dma((NZ,)),
            dma((NZ, NX)), dma((NZ, NX)),
            dma((NKV,)), dma((NKV,)),
        ],
        compiler_params=pltpu.CompilerParams(
            collective_id=0, has_side_effects=True, vmem_limit_bytes=40 * 1024 * 1024
        ),
        name="star",
    )(ctx_query, ctx_kv, new_query, new_kv, out_weight)


def solution(mesh):
    return jax.shard_map(
        body,
        mesh=mesh,
        in_specs=(
            P("kv", "ctx", None),
            P(None, "kv", "ctx", None),
            P("kv", "ctx", None),
            P(None, "kv", "ctx", None),
            P("kv", "ctx"),
        ),
        out_specs=(P("kv", "ctx", None), P("kv", "ctx")),
        check_vma=False,
    )
```

time: 546 us -> 69.9 us (0.13)
  waiting for transfers between devices: 248 us -> 0 us
  blocking collectives: 115 us -> 0 us
  other arithmetic: 100 us -> 0 us
  Pallas kernels: 0 us -> 62.7 us
  matrix products: 33.8 us -> 0 us
  local copies, waits for them, and re-layouts: 29.7 us -> 6.19 us
  between operations: 14.2 us -> 0.65 us
    all_gather x1 -> x0, waiting for transfers between devices: 209 us -> none  [merged_2(): pieces = jax.tree.map(lambda part: lax.all_gather(part, axis), value)]
    all_gather x3 -> x0, blocking collectives: 115 us -> none  [the longest x2 72 us: merged_2(): pieces = jax.tree.map(lambda part: lax.all_gather(part, axis), value)]
    add x63 -> x0, other arithmetic: 88.1 us -> none  [the longest x31 66 us: combine(): first[2] * left[..., None] + second[2] * right[..., None]]
    pallas_call x0 -> x1, Pallas kernels: none -> 62.7 us  [body(): pl.pallas_call(kernel, out_shape=(jax.ShapeDtypeStruct(ctx_query.shape, B...]
    dot_general x33 -> x0, matrix products: 33.8 us -> none  [the longest x16 21.2 us: stats(): jnp.dot(weights.astype(jnp.bfloat16), values, preferred_element_type=jnp....]
    slice x9 -> x0, local copies, waits for them, and re-layouts: 23.6 us -> none  [the longest x3 23.6 us: merged_2(): tail = jax.tree.map(lambda part: part[1:], pieces)]
    reduce_scatter x1 -> x0, waiting for transfers between devices: 21.3 us -> none  [body(): lax.psum_scatter(jnp.dot(everyone, out_weight, preferred_element_type=jnp...]
    psum x1 -> x0, waiting for transfers between devices: 18.4 us -> none  [spread(): return lax.psum(jnp.where(mine, shard, jnp.zeros_like(shard)), axis)]
  transfers between devices with their start and end apart: 3 -> 0, of which waited for: 3 -> 0; matrix products, arithmetic and copies ran while one was open for 9% -> 0% of each run, Pallas kernels for 0% -> 0%
where the time goes in v1:
time: 69.9 us; the launch traced here: 69.6 us
  Pallas kernels  62.7 us (90%)
  local copies, waits for them, and re-layouts  6.19 us (9%)
    pallas_call x1, Pallas kernels, body(): pl.pallas_call(kernel, out_shape=(jax.ShapeDtypeStruct(ctx_query.shape, B...  62.7 us
    unnamed x12, local copies, waits for them, and re-layouts  6.19 us

profile of v1, /device:TPU:1, one launch (start us, length us, event | category | flops | bytes accessed | tf_op | source)
XLA Modules:
  0.0 69.6 jit_solution(16624905522449409177)
XLA Ops:
  0.6 0.0 copy-start
  0.6 1.2 %copy-done = bf16[1,512,1024]{2,1,0:T(8,128)(2,1)S(1)} copy-done((bf16[1,512,1024]{2,1,0:T(8,128)(2,1)S(1)}, bf16[1,512,1024]{2,1,0:T(8,128)(2,1)}, u32[]{:S(2)}) %copy-start) | copy-done | bytes 1048600
  1.9 0.0 copy-start.1
  1.9 1.0 %copy-done.1 = bf16[1024,256]{1,0:T(8,128)(2,1)S(1)} copy-done((bf16[1024,256]{1,0:T(8,128)(2,1)S(1)}, bf16[1024,256]{1,0:T(8,128)(2,1)}, u32[]{:S(2)}) %copy-start.1) | copy-done | bytes 524312
  2.9 0.0 copy-start.2
  2.9 0.9 %copy-done.2 = bf16[2,1,512,128]{3,2,1,0:T(8,128)(2,1)S(1)} copy-done((bf16[2,1,512,128]{3,2,1,0:T(8,128)(2,1)S(1)}, bf16[2,1,512,128]{3,2,1,0:T(8,128)(2,1)}, u32[]{:S(2)}) %copy-start.2) | copy-done | bytes 262168
  3.8 0.0 copy-start.3
  3.9 0.7 %copy-done.3 = bf16[1,8,1024]{2,1,0:T(8,128)(2,1)S(1)} copy-done((bf16[1,8,1024]{2,1,0:T(8,128)(2,1)S(1)}, bf16[1,8,1024]{2,1,0:T(8,128)(2,1)}, u32[]{:S(2)}) %copy-start.3) | copy-done | bytes 16408
  4.6 0.0 copy-start.4
  4.6 0.7 copy-done.4
  5.3 62.7 %star.1 = (bf16[1,512,1024]{2,1,0:T(8,128)(2,1)S(1)}, bf16[32,256]{1,0:T(8,128)(2,1)S(1)}) custom-call(bf16[1,512,1024]{2,1,0:T(8,128)(2,1)S(1)} %copy-done, bf16[2,1,512,128]{3,2,1,0:T(8,128)(2,1)S(1)} %copy-done.2, bf16[1,8,1024]{2,1,0:T(8,128)(2,1)S(1)} %copy-done.3, bf16[2,1,8,128]{3,2,1,0:T(8,128)(2,1)S(1)} %copy-done.4, bf16[1024,256]{1,0:T(8,128)(2,1)S(1)} %copy-done.1), custom_call_target="tpu_custom_call" | custom-call | tf_op jit(solution)/shard_map/star/pallas_call | solution.py:301
  68.0 1.0 %copy.9 = bf16[1,512,1024]{2,1,0:T(8,128)(2,1)} copy(bf16[1,512,1024]{2,1,0:T(8,128)(2,1)S(1)} %get-tuple-element.4) | data formatting | bytes 2097152
  69.0 0.6 copy.10
Async XLA Ops:
  0.6 1.2 %copy-start = (bf16[1,512,1024]{2,1,0:T(8,128)(2,1)S(1)}, bf16[1,512,1024]{2,1,0:T(8,128)(2,1)}, u32[]{:S(2)}) copy-start(bf16[1,512,1024]{2,1,0:T(8,128)(2,1)} %cq_h.1) | copy-start | bytes 3145732
  1.9 1.0 %copy-start.1 = (bf16[1024,256]{1,0:T(8,128)(2,1)S(1)}, bf16[1024,256]{1,0:T(8,128)(2,1)}, u32[]{:S(2)}) copy-start(bf16[1024,256]{1,0:T(8,128)(2,1)} %w_h.1) | copy-start | bytes 1572868
  2.9 0.9 %copy-start.2 = (bf16[2,1,512,128]{3,2,1,0:T(8,128)(2,1)S(1)}, bf16[2,1,512,128]{3,2,1,0:T(8,128)(2,1)}, u32[]{:S(2)}) copy-start(bf16[2,1,512,128]{3,2,1,0:T(8,128)(2,1)} %ckv_h.1) | copy-start | bytes 786436
  3.8 0.7 %copy-start.3 = (bf16[1,8,1024]{2,1,0:T(8,128)(2,1)S(1)}, bf16[1,8,1024]{2,1,0:T(8,128)(2,1)}, u32[]{:S(2)}) copy-start(bf16[1,8,1024]{2,1,0:T(8,128)(2,1)} %nq_ref.1) | copy-start | bytes 49156
  4.6 0.7 copy-start.4

commit v2 on v1

--- a/solution.py
+++ b/solution.py
@@ -35,7 +35,7 @@
 
 
 def scores(q, k):
-    return lax.dot_general(q, k, (((1,), (1,)), ((), ())), preferred_element_type=F32) * SCALE
+    return lax.dot_general(q, k, (((1,), (1,)), ((), ())), preferred_element_type=F32)
 
 
 def with_ones(v):
@@ -43,7 +43,11 @@
 
 
 def weigh(s, top, v1):
-    return jnp.dot(jnp.exp2(s - top).astype(BF16), v1, preferred_element_type=F32)
+    return jnp.dot(jnp.exp2((s - top) * SCALE).astype(BF16), v1, preferred_element_type=F32)
+
+
+def peak_of(s):
+    return jnp.max(s, axis=1, keepdims=True)
 
 
 def kernel(
@@ -87,78 +91,100 @@
     for d in ZS:
         q_copies[d].start()
     kv_copies = {}
+
+    def send_kv(name, src, dst, dev):
+        kv_copies[name] = rcopy(src, dst, kv_ss.at[len(kv_copies)], kv_rs.at[len(kv_copies)], dev)
+        kv_copies[name].start()
+
+    for e in XS:
+        send_kv(("fresh", e), fresh.at[0], fresh.at[e], xdev(e))
     for part in range(2):
-        for e in XS:
-            kv_copies[e, part] = rcopy(
-                ckv_h.at[part, 0], kv.at[e, part], kv_ss.at[part, e], kv_rs.at[part, e], xdev(e)
-            )
-            kv_copies[e, part].start()
-        if part == 0:
-            for e in XS:
-                kv_copies[e, 2] = rcopy(
-                    fresh.at[0], fresh.at[e], kv_ss.at[2, e], kv_rs.at[2, e], xdev(e)
-                )
-                kv_copies[e, 2].start()
+        for e in (1, 3):
+            send_kv((part, e), ckv_h.at[part, 0], kv.at[e, part], xdev(e))
+
+    def pass_on(part):
+        for e in (1, 3):
+            half = pl.ds((e // 2) * (BLK // 2), BLK // 2)
+            kv_copies[part, e].wait_recv()
+            send_kv((part, 2, e), kv.at[e, part, half], kv.at[2, part, half], xdev(e))
 
     load_kv.wait()
     load_cq.wait()
 
+    keep = lax.broadcasted_iota(jnp.int32, (128, 128), 1) <= lax.broadcasted_iota(
+        jnp.int32, (128, 128), 0
+    )
+
     def own_head(g, carry):
         cols = pl.ds(pl.multiple_of(g * HD, HD), HD)
-        for r in range(4):
-            width = (r + 1) * 128
-            q = cq[pl.ds(r * 128, 128), cols]
-            s = scores(q, kv[0, 0, pl.ds(0, width), :])
-            row = lax.broadcasted_iota(jnp.int32, (128, width), 0) + r * 128
-            col = lax.broadcasted_iota(jnp.int32, (128, width), 1)
-            s = jnp.where(col <= row, s, LOW)
-            top = jnp.max(s, axis=1, keepdims=True)
-            own_n[g, pl.ds(r * 128, 128), :] = weigh(s, top, with_ones(kv[0, 1, pl.ds(0, width), :]))
-            own_m[g, pl.ds(r * 128, 128), :] = jnp.broadcast_to(top, (128, HD))
+        tiles = [pl.ds(r * 128, 128) for r in range(4)]
+        found = [
+            scores(cq[at, cols], kv[0, 0, pl.ds(0, (r + 1) * 128), :]) for r, at in enumerate(tiles)
+        ]
+        weights = []
+        for r, at in enumerate(tiles):
+            s = jnp.where(keep, found[r][:, r * 128 :], LOW)
+            if r:
+                s = jnp.concatenate([found[r][:, : r * 128], s], 1)
+            top = peak_of(s)
+            weights.append(jnp.exp2((s - top) * SCALE).astype(BF16))
+            own_m[g, at, :] = jnp.broadcast_to(top, (128, HD))
+        for r, at in enumerate(tiles):
+            v1 = with_ones(kv[0, 1, pl.ds(0, (r + 1) * 128), :])
+            own_n[g, at, :] = jnp.dot(weights[r], v1, preferred_element_type=F32)
         return carry
 
-    lax.fori_loop(0, GROUP, own_head, 0)
-
+    lax.fori_loop(0, GROUP, own_head, 0, unroll=4)
+
+    pass_on(0)
     for d in ZS:
         q_copies[d].wait_recv()
-
-    def query_block(e):
-        def rows(c, carry):
-            at = pl.ds(pl.multiple_of(c * 128, 128), 128)
-            q = qbuf[pl.ds(c * 2, 2)].reshape(128, HD)
-            s = scores(q, kv[e, 0])
-            top = jnp.max(s, axis=1, keepdims=True)
-            if e == 0:
-                q_n[at, :] = weigh(s, top, with_ones(kv[e, 1]))
-            else:
-                old = q_m[at, :][:, :1]
-                top = jnp.maximum(top, old)
-                q_n[at, :] = q_n[at, :] * jnp.exp2(old - top) + weigh(s, top, with_ones(kv[e, 1]))
-            q_m[at, :] = jnp.broadcast_to(top, (128, HD))
-            return carry
-
-        lax.fori_loop(0, NZ * ROWS // 128, rows, 0)
-
-    query_block(0)
     for e in XS:
-        kv_copies[e, 0].wait_recv()
-        kv_copies[e, 1].wait_recv()
-        query_block(e)
-    for e in XS:
-        kv_copies[e, 2].wait_recv()
-
-    q = qbuf[...].reshape(NZ * ROWS, HD)
-    s = scores(q, fresh[:, 0].reshape(NX * 16, HD))
-    row = lax.broadcasted_iota(jnp.int32, s.shape, 0)
-    col = lax.broadcasted_iota(jnp.int32, s.shape, 1)
-    token = (x * NZ + (z - row // ROWS + NZ) % NZ) * QT + row % QT
+        kv_copies["fresh", e].wait_recv()
+
+    row = lax.broadcasted_iota(jnp.int32, (128, NX * 16), 0)
+    col = lax.broadcasted_iota(jnp.int32, (128, NX * 16), 1)
     key = ((x - col // 16 + NX) % NX * NZ + z) * QT + col % 16
-    s = jnp.where((col % 16 < QT) & (key <= token), s, LOW)
-    old = q_m[...][:, :1]
-    top = jnp.maximum(jnp.max(s, axis=1, keepdims=True), old)
-    total = q_n[...] * jnp.exp2(old - top) + weigh(s, top, with_ones(fresh[:, 1].reshape(NX * 16, HD)))
-    n_send[...] = (total[:, :HD] / total[:, HD:]).astype(BF16).reshape(NZ, ROWS, HD)
-    lse = (top + jnp.log2(total[:, HD:])).reshape(NZ, GROUP, QT, HD)
+    chunks = range(NZ * ROWS // 128)
+    rows = [pl.ds(c * 128, 128) for c in chunks]
+    qs = [qbuf[pl.ds(c * 2, 2)].reshape(128, HD) for c in chunks]
+    fresh_k = fresh[:, 0].reshape(NX * 16, HD)
+    fresh_v = with_ones(fresh[:, 1].reshape(NX * 16, HD))
+    found = [(scores(q, fresh_k), scores(q, kv[0, 0])) for q in qs]
+    tops = []
+    for c in chunks:
+        token = (x * NZ + (z - c * 2 - row // ROWS + NZ) % NZ) * QT + row % QT
+        s = jnp.where((col % 16 < QT) & (key <= token), found[c][0], LOW)
+        top = jnp.maximum(peak_of(s), peak_of(found[c][1]))
+        q_n[rows[c], :] = weigh(s, top, fresh_v) + weigh(found[c][1], top, with_ones(kv[0, 1]))
+        q_m[rows[c], :] = jnp.broadcast_to(top, (128, HD))
+
+    pass_on(1)
+    found = [(scores(q, kv[1, 0]), scores(q, kv[3, 0])) for q in qs]
+    for c in chunks:
+        old = q_m[rows[c], :][:, :1]
+        top = jnp.maximum(jnp.maximum(old, peak_of(found[c][0])), peak_of(found[c][1]))
+        fade = jnp.exp2((old - top) * SCALE)
+        q_n[rows[c], :] = (
+            q_n[rows[c], :] * fade
+            + weigh(found[c][0], top, with_ones(kv[1, 1]))
+            + weigh(found[c][1], top, with_ones(kv[3, 1]))
+        )
+        q_m[rows[c], :] = jnp.broadcast_to(top, (128, HD))
+
+    for part in range(2):
+        for e in (1, 3):
+            kv_copies[part, 2, e].wait_recv()
+    found = [scores(q, kv[2, 0]) for q in qs]
+    totals, lses = [], []
+    for c in chunks:
+        old = q_m[rows[c], :][:, :1]
+        top = jnp.maximum(old, peak_of(found[c]))
+        n = q_n[rows[c], :] * jnp.exp2((old - top) * SCALE) + weigh(found[c], top, with_ones(kv[2, 1]))
+        totals.append(n[:, :HD] / n[:, HD:])
+        lses.append(top * SCALE + jnp.log2(n[:, HD:]))
+    lse = jnp.concatenate(lses, 0).reshape(NZ, GROUP, QT, HD)
+    n_send[...] = jnp.concatenate(totals, 0).astype(BF16).reshape(NZ, ROWS, HD)
     lane = lax.broadcasted_iota(jnp.int32, (NZ, QT, HD), 2)
     stat = jnp.full((NZ, QT, HD), 0.0, F32)
     for g in range(GROUP):
@@ -188,13 +214,6 @@
     @pl.when(z > 0)
     def _():
         rcopy(piece(kv.at[0], 0), piece(anc, z), sc_ss.at[0], sc_rs, zdev(1)).wait_recv()
-
-    spreads = {d: rcopy(piece(anc, z), piece(anc, z), an_ss.at[d], an_rs.at[d], zdev(d)) for d in ZS}
-    for d in ZS:
-
-        @pl.when((z + d) % NZ != 0)
-        def _():
-            spreads[d].start()
 
     for c in n_copies:
         c.wait_recv()
@@ -222,9 +241,48 @@
             ax[d, e].start()
 
     forward(0)
+    spreads = {d: rcopy(piece(anc, z), piece(anc, z), an_ss.at[d], an_rs.at[d], zdev(d)) for d in ZS}
+    for d in ZS:
+
+        @pl.when((z + d) % NZ != 0)
+        def _():
+            spreads[d].start()
+
     for d in ZS:
         az[d].wait_recv()
         forward(d)
+
+    load_w.wait()
+    mine = NCTX * QT // NKV
+    po_copies = {}
+
+    def project(e):
+        block = (x - e + NX) % NX
+        lhs = att[pl.ds(block * NZ, NZ)].astype(F32)
+        acc = jnp.zeros((NZ * QT, no_ref.shape[1]), F32)
+        for j in range(GROUP // 2):
+            pair = [lhs[:, g * QT : (g + 1) * QT].reshape(NZ * QT, HD) for g in (2 * j, 2 * j + 1)]
+            acc = acc + jnp.dot(
+                jnp.concatenate(pair, 1).astype(BF16),
+                w[pl.ds(j * 2 * HD, 2 * HD), :],
+                preferred_element_type=F32,
+            )
+        po[pl.ds(block * NC, NC)] = acc.reshape(NC, mine, acc.shape[1])
+        for c in range(NC):
+            dest = block * NC + c
+            po_copies[e, c] = rcopy(
+                po.at[dest], po_recv.at[head], po_ss.at[e * NC + c], po_rs.at[head], (here, dest)
+            )
+
+            @pl.when(dest != head)
+            def _():
+                po_copies[e, c].start()
+
+    project(0)
+    for e in XS:
+        for d in (0,) + ZS:
+            ax[d, e].wait_recv()
+        project(e)
 
     @pl.when(z > 0)
     def _():
@@ -236,48 +294,40 @@
         for r in range(4):
             at = pl.ds(r * 128, 128)
             s = scores(cq[at, cols], anc[0])
-            top = jnp.max(s, axis=1, keepdims=True)
+            top = peak_of(s)
             n = weigh(s, top, with_ones(anc[1]))
             old = own_m[g, at, :]
             peak = jnp.maximum(old, top)
-            mine = jnp.where(here > 0, jnp.exp2(old - peak), 1.0)
-            theirs = jnp.where(here > 0, jnp.exp2(top - peak), 0.0)
+            mine = jnp.where(here > 0, jnp.exp2((old - peak) * SCALE), 1.0)
+            theirs = jnp.where(here > 0, jnp.exp2((top - peak) * SCALE), 0.0)
             summed = own_n[g, at, :]
             total = summed[:, HD:] * mine + n[:, HD:] * theirs
             out[at, cols] = ((summed[:, :HD] * mine + n[:, :HD] * theirs) / total).astype(BF16)
         return carry
 
-    lax.fori_loop(0, GROUP, anchor_head, 0)
+    lax.fori_loop(0, GROUP, anchor_head, 0, unroll=4)
     store_out = pltpu.make_async_copy(out, co_h.at[0], loc.at[4])
     store_out.start()
 
-    load_w.wait()
-    for c in ax.values():
-        c.wait_recv()
-    acc = jnp.zeros((NCTX * QT, no_ref.shape[1]), F32)
-    for j in range(GROUP // 2):
-        pair = att[:, pl.ds(j * 16, 16), :].astype(F32)
-        lhs = jnp.concatenate(
-            [pair[:, :QT].reshape(NCTX * QT, HD), pair[:, QT:].reshape(NCTX * QT, HD)], 1
-        ).astype(BF16)
-        acc = acc + jnp.dot(lhs, w[pl.ds(j * 256, 256), :], preferred_element_type=F32)
-    po[...] = acc.reshape(po.shape)
-    po_copies = []
-    for i, (dy, dc) in enumerate(KVS):
-        dest = (y + dy) % NY * NC + (co + dc) % NC
-        po_copies.append(rcopy(po.at[dest], po_recv.at[i], po_ss.at[i], po_rs.at[i], (here, dest)))
-        po_copies[i].start()
     total = po[head]
-    for i, c in enumerate(po_copies):
-        c.wait_recv()
-        total = total + po_recv[i]
+    for dy, dc in KVS:
+        source = (y + dy) % NY * NC + (co + dc) % NC
+        rcopy(po.at[0], po_recv.at[source], po_ss.at[0], po_rs.at[source], (here, source)).wait_recv()
+        total = total + po_recv[source]
     no_ref[...] = total.astype(BF16)
 
     for group in (q_copies, kv_copies, az, ax):
         for c in group.values():
             c.wait_send()
-    for c in n_copies + po_copies:
+    for c in n_copies:
         c.wait_send()
+    for e in range(NX):
+        for c in range(NC):
+
+            @pl.when((x - e + NX) % NX * NC + c != head)
+            def _():
+                po_copies[e, c].wait_send()
+
     for d in ZS:
 
         @pl.when((z + d) % NZ != 0)
@@ -293,7 +343,7 @@
 
 
 def body(ctx_query, ctx_kv, new_query, new_kv, out_weight):
-    any_space = pl.BlockSpec(memory_space=pl.ANY)
+    any_space = pl.BlockSpec(memory_space=pltpu.HBM)
     vmem = pl.BlockSpec(memory_space=pltpu.VMEM)
     cols = out_weight.shape[1]
     mine = NCTX * QT // NKV
@@ -324,10 +374,10 @@
             pltpu.VMEM((NZ, QT, HD), F32),
             pltpu.VMEM((NCTX, ROWS, HD), BF16),
             pltpu.VMEM((NKV, mine, cols), F32),
-            pltpu.VMEM((NKV - 1, mine, cols), F32),
+            pltpu.VMEM((NKV, mine, cols), F32),
             dma((5,)),
             dma((NZ,)), dma((NZ,)),
-            dma((3, NX)), dma((3, NX)),
+            dma((11,)), dma((11,)),
             dma((2, NZ)), dma((2, NZ)),
             dma((NZ,)), dma((NZ,)),
             dma((NZ,)), dma,
@@ -336,7 +386,7 @@
             dma((NKV,)), dma((NKV,)),
         ],
         compiler_params=pltpu.CompilerParams(
-            collective_id=0, has_side_effects=True, vmem_limit_bytes=40 * 1024 * 1024
+            collective_id=0, has_side_effects=True, vmem_limit_bytes=60 * 1024 * 1024
         ),
         name="star",
     )(ctx_query, ctx_kv, new_query, new_kv, out_weight)

time: 69.9 us -> 55.8 us (0.80)
  the two profiles are of different devices: /device:TPU:1 before, /device:TPU:5 now
where the time goes in v2:
time: 55.8 us; the launch traced here: 55.6 us
  Pallas kernels  52.1 us (93%)
  local copies, waits for them, and re-layouts  2.88 us (5%)
  between operations  0.65 us (1%)
    pallas_call x1, Pallas kernels, body(): pl.pallas_call(kernel, out_shape=(jax.ShapeDtypeStruct(ctx_query.shape, B...  52.1 us
    unnamed x4, local copies, waits for them, and re-layouts  2.88 us

profile of v2, /device:TPU:5, one launch (start us, length us, event | category | flops | bytes accessed | tf_op | source)
XLA Modules:
  0.0 55.6 jit_solution(6014573749876357686)
XLA Ops:
  0.6 52.1 %star.1 = (bf16[1,512,1024]{2,1,0:T(8,128)(2,1)}, bf16[32,256]{1,0:T(8,128)(2,1)}) custom-call(bf16[1,512,1024]{2,1,0:T(8,128)(2,1)} %cq_h.1, bf16[2,1,512,128]{3,2,1,0:T(8,128)(2,1)} %ckv_h.1, bf16[1,8,1024]{2,1,0:T(8,128)(2,1)} %nq_ref.1, bf16[2,1,8,128]{3,2,1,0:T(8,128)(2,1)} %nkv_ref.1, bf16[1024,256]{1,0:T(8,128)(2,1)} %w_h.1), custom_call_target="tpu_custom_call" | custom-call | tf_op jit(solution)/shard_map/star/pallas_call | solution.py:351
  52.7 0.0 copy-start
  52.7 2.3 %copy.9 = bf16[1,512,1024]{2,1,0:T(8,128)(2,1)} copy(bf16[1,512,1024]{2,1,0:T(8,128)(2,1)} %get-tuple-element.4) | data formatting | bytes 2097152
  55.0 0.0 copy-done
  55.0 0.6 %copy.10 = bf16[32,256]{1,0:T(8,128)(2,1)} copy(bf16[32,256]{1,0:T(8,128)(2,1)S(1)} %copy-done) | data formatting | bytes 32768
Async XLA Ops:
  52.7 2.3 %copy-start = (bf16[32,256]{1,0:T(8,128)(2,1)S(1)}, bf16[32,256]{1,0:T(8,128)(2,1)}, u32[]{:S(2)}) copy-start(bf16[32,256]{1,0:T(8,128)(2,1)} %get-tuple-element.5) | copy-start | bytes 49156

commit v3 on v2

--- a/solution.py
+++ b/solution.py
@@ -14,11 +14,13 @@
 NCTX, NKV = NX * NZ, NY * NC
 QT = 8
 ROWS = QT * GROUP
-PIECE = BLK // NZ
+STRIPE = BLK // NX
+PIECE = STRIPE // NZ
 SCALE = HD**-0.5 * math.log2(math.e)
 LOW = -1e30
 ZS = (1, 7, 2, 6, 3, 5, 4)
-XS = (1, 3, 2)
+FAR = ZS[::-1]
+SIDES = (1, 3, 2)
 KVS = ((0, 1), (1, 0), (3, 0), (1, 1), (3, 1), (2, 0), (2, 1))
 F32, BF16 = jnp.float32, jnp.bfloat16
 
@@ -55,24 +57,31 @@
     co_h, no_ref,
     cq, kv, w, fresh, qbuf, anc, own_n, own_m, out, q_n, q_m,
     n_send, n_recv, st_send, st_recv, att, po, po_recv,
-    loc, q_ss, q_rs, kv_ss, kv_rs, n_ss, n_rs, an_ss, an_rs, sc_ss, sc_rs,
+    loc, q_ss, q_rs, kv_ss, kv_rs, n_ss, n_rs, an_ss, an_rs, sc_ss, sc_rs, pass_ss, pass_rs, st_ss, st_rs,
     az_ss, az_rs, ax_ss, ax_rs, po_ss, po_rs,
 ):
     here = lax.axis_index("ctx")
     head = lax.axis_index("kv")
     x, z, y, co = here // NZ, here % NZ, head // NC, head % NC
 
+    def member(d):
+        return (x + 2 * (d % 2)) % NX * NZ + (z + d) % NZ
+
+    colour = (x + 2 * (z % 2)) % NX
+
     def zdev(d):
-        return (x * NZ + (z + d) % NZ, head)
-
-    def xdev(e):
-        return ((x + e) % NX * NZ + z, head)
+        return (member(d), head)
+
+    def side(e):
+        if e % 2:
+            return ((x + e) % NX * NZ + z, head)
+        return (x * NZ + (z + (1 if e == 2 else NZ - 1)) % NZ, head)
 
     def kvdev(dy, dc):
         return (here, (y + dy) % NY * NC + (co + dc) % NC)
 
     barrier = pltpu.get_barrier_semaphore()
-    peers = [zdev(d) for d in ZS] + [xdev(e) for e in XS] + [kvdev(*k) for k in KVS]
+    peers = [zdev(d) for d in ZS] + [side(e) for e in (1, 3, 2, 4)] + [kvdev(*k) for k in KVS]
     for dev in peers:
         pl.semaphore_signal(barrier, inc=1, device_id=dev, device_id_type=pl.DeviceIdType.MESH)
     load_kv = pltpu.make_async_copy(ckv_h.at[:, 0], kv.at[0], loc.at[0])
@@ -88,7 +97,7 @@
     pl.semaphore_wait(barrier, len(peers))
 
     q_copies = {d: rcopy(qbuf.at[0], qbuf.at[d], q_ss.at[d], q_rs.at[d], zdev(d)) for d in ZS}
-    for d in ZS:
+    for d in FAR:
         q_copies[d].start()
     kv_copies = {}
 
@@ -96,17 +105,14 @@
         kv_copies[name] = rcopy(src, dst, kv_ss.at[len(kv_copies)], kv_rs.at[len(kv_copies)], dev)
         kv_copies[name].start()
 
-    for e in XS:
-        send_kv(("fresh", e), fresh.at[0], fresh.at[e], xdev(e))
+    for e in SIDES:
+        send_kv(("fresh", e), fresh.at[0], fresh.at[e], side(e))
     for part in range(2):
         for e in (1, 3):
-            send_kv((part, e), ckv_h.at[part, 0], kv.at[e, part], xdev(e))
-
-    def pass_on(part):
-        for e in (1, 3):
-            half = pl.ds((e // 2) * (BLK // 2), BLK // 2)
-            kv_copies[part, e].wait_recv()
-            send_kv((part, 2, e), kv.at[e, part, half], kv.at[2, part, half], xdev(e))
+            send_kv((part, e), ckv_h.at[part, 0], kv.at[e, part], side(e))
+        for e in (2, 4):
+            half = pl.ds((e // 2 - 1) * (BLK // 2), BLK // 2)
+            send_kv((part, e), ckv_h.at[part, 0, half], kv.at[2, part, half], side(e))
 
     load_kv.wait()
     load_cq.wait()
@@ -136,51 +142,69 @@
 
     lax.fori_loop(0, GROUP, own_head, 0, unroll=4)
 
-    pass_on(0)
     for d in ZS:
         q_copies[d].wait_recv()
-    for e in XS:
+    for e in SIDES:
         kv_copies["fresh", e].wait_recv()
+    for part in range(2):
+        for e in (2, 4):
+            kv_copies[part, e].wait_recv()
 
     row = lax.broadcasted_iota(jnp.int32, (128, NX * 16), 0)
     col = lax.broadcasted_iota(jnp.int32, (128, NX * 16), 1)
-    key = ((x - col // 16 + NX) % NX * NZ + z) * QT + col % 16
+    slot = col // 16
+    key_x = jnp.where(slot == 2, x, (x - slot + NX) % NX)
+    key_z = jnp.where(slot == 2, (z + NZ - 1) % NZ, z)
+    key = (key_x * NZ + key_z) * QT + col % 16
     chunks = range(NZ * ROWS // 128)
     rows = [pl.ds(c * 128, 128) for c in chunks]
     qs = [qbuf[pl.ds(c * 2, 2)].reshape(128, HD) for c in chunks]
     fresh_k = fresh[:, 0].reshape(NX * 16, HD)
     fresh_v = with_ones(fresh[:, 1].reshape(NX * 16, HD))
-    found = [(scores(q, fresh_k), scores(q, kv[0, 0])) for q in qs]
-    tops = []
+    found = [(scores(q, fresh_k), scores(q, kv[0, 0]), scores(q, kv[2, 0])) for q in qs]
     for c in chunks:
-        token = (x * NZ + (z - c * 2 - row // ROWS + NZ) % NZ) * QT + row % QT
+        came = c * 2 + row // ROWS
+        token = ((x + 2 * (came % 2)) % NX * NZ + (z - came + NZ) % NZ) * QT + row % QT
         s = jnp.where((col % 16 < QT) & (key <= token), found[c][0], LOW)
-        top = jnp.maximum(peak_of(s), peak_of(found[c][1]))
-        q_n[rows[c], :] = weigh(s, top, fresh_v) + weigh(found[c][1], top, with_ones(kv[0, 1]))
+        top = jnp.maximum(jnp.maximum(peak_of(s), peak_of(found[c][1])), peak_of(found[c][2]))
+        q_n[rows[c], :] = (
+            weigh(s, top, fresh_v)
+            + weigh(found[c][1], top, with_ones(kv[0, 1]))
+            + weigh(found[c][2], top, with_ones(kv[2, 1]))
+        )
         q_m[rows[c], :] = jnp.broadcast_to(top, (128, HD))
 
-    pass_on(1)
+    for part in range(2):
+        for e in (1, 3):
+            kv_copies[part, e].wait_recv()
+
+    def stripe(ref, k):
+        return ref.at[:, pl.ds(pl.multiple_of(k * STRIPE, STRIPE), STRIPE)]
+
+    def piece(p):
+        return anc.at[:, pl.ds(pl.multiple_of(colour * STRIPE + p * PIECE, PIECE), PIECE)]
+
+    local_stripe = pltpu.make_async_copy(stripe(kv.at[x], x), stripe(anc, x), loc.at[3])
+    far_stripe = rcopy(stripe(kv.at[1], 2), stripe(anc, 2), pass_ss, pass_rs, side(1))
+
+    @pl.when((z == 0) & (x != 2))
+    def _():
+        local_stripe.start()
+
+    @pl.when(here == NZ)
+    def _():
+        far_stripe.start()
+
     found = [(scores(q, kv[1, 0]), scores(q, kv[3, 0])) for q in qs]
+    totals, lses = [], []
     for c in chunks:
         old = q_m[rows[c], :][:, :1]
         top = jnp.maximum(jnp.maximum(old, peak_of(found[c][0])), peak_of(found[c][1]))
-        fade = jnp.exp2((old - top) * SCALE)
-        q_n[rows[c], :] = (
-            q_n[rows[c], :] * fade
+        n = (
+            q_n[rows[c], :] * jnp.exp2((old - top) * SCALE)
             + weigh(found[c][0], top, with_ones(kv[1, 1]))
             + weigh(found[c][1], top, with_ones(kv[3, 1]))
         )
-        q_m[rows[c], :] = jnp.broadcast_to(top, (128, HD))
-
-    for part in range(2):
-        for e in (1, 3):
-            kv_copies[part, 2, e].wait_recv()
-    found = [scores(q, kv[2, 0]) for q in qs]
-    totals, lses = [], []
-    for c in chunks:
-        old = q_m[rows[c], :][:, :1]
-        top = jnp.maximum(old, peak_of(found[c]))
-        n = q_n[rows[c], :] * jnp.exp2((old - top) * SCALE) + weigh(found[c], top, with_ones(kv[2, 1]))
         totals.append(n[:, :HD] / n[:, HD:])
         lses.append(top * SCALE + jnp.log2(n[:, HD:]))
     lse = jnp.concatenate(lses, 0).reshape(NZ, GROUP, QT, HD)
@@ -192,28 +216,26 @@
     st_send[...] = stat
 
     n_copies = []
-    for d in ZS:
+    for d in FAR:
         n_copies.append(rcopy(st_send.at[d], st_recv.at[d], n_ss.at[0, d], n_rs.at[0, d], zdev(NZ - d)))
         n_copies.append(rcopy(n_send.at[d], n_recv.at[d], n_ss.at[1, d], n_rs.at[1, d], zdev(NZ - d)))
     for c in n_copies:
         c.start()
 
-    def piece(ref, p):
-        return ref.at[:, pl.ds(pl.multiple_of(p * PIECE, PIECE), PIECE)]
-
-    local_anchor = pltpu.make_async_copy(kv.at[x], anc, loc.at[3])
-    scatters = [rcopy(piece(kv.at[x], p), piece(anc, p), sc_ss.at[p], sc_rs, zdev(p)) for p in range(1, NZ)]
+    scatters = [rcopy(piece(p), piece(p), sc_ss.at[p], sc_rs, zdev(p)) for p in range(1, NZ)]
+
+    @pl.when((z == 0) & (x != 2))
+    def _():
+        local_stripe.wait()
+
+    @pl.when(here == 2 * NZ)
+    def _():
+        far_stripe.wait_recv()
 
     @pl.when(z == 0)
     def _():
         for c in scatters:
             c.start()
-        local_anchor.start()
-        local_anchor.wait()
-
-    @pl.when(z > 0)
-    def _():
-        rcopy(piece(kv.at[0], 0), piece(anc, z), sc_ss.at[0], sc_rs, zdev(1)).wait_recv()
 
     for c in n_copies:
         c.wait_recv()
@@ -230,19 +252,25 @@
     att[here] = jnp.concatenate(pieces, 0).astype(BF16)
 
     az = {d: rcopy(att.at[here], att.at[here], az_ss.at[d], az_rs.at[d], zdev(d)) for d in ZS}
-    for d in ZS:
+    for d in FAR:
         az[d].start()
     ax = {}
 
     def forward(d):
-        block = x * NZ + (z - d + NZ) % NZ
-        for e in XS:
-            ax[d, e] = rcopy(att.at[block], att.at[block], ax_ss.at[d, e], ax_rs.at[d, e], xdev(e))
+        block = member(NZ - d)
+        for e in SIDES:
+            dev = side(4) if e == 2 and d % 2 else side(e)
+            ax[d, e] = rcopy(att.at[block], att.at[block], ax_ss.at[d, e], ax_rs.at[d, e], dev)
             ax[d, e].start()
 
     forward(0)
-    spreads = {d: rcopy(piece(anc, z), piece(anc, z), an_ss.at[d], an_rs.at[d], zdev(d)) for d in ZS}
-    for d in ZS:
+
+    @pl.when(z > 0)
+    def _():
+        rcopy(piece(0), piece(z), sc_ss.at[0], sc_rs, zdev(1)).wait_recv()
+
+    spreads = {d: rcopy(piece(z), piece(z), an_ss.at[d], an_rs.at[d], zdev(d)) for d in ZS}
+    for d in FAR:
 
         @pl.when((z + d) % NZ != 0)
         def _():
@@ -251,6 +279,22 @@
     for d in ZS:
         az[d].wait_recv()
         forward(d)
+
+    @pl.when(z > 0)
+    def _():
+        for d in ZS:
+            spreads[d].wait_recv()
+
+    stripes = []
+    for e in (1, 3):
+        mine = stripe(anc, colour)
+        stripes.append(rcopy(mine, mine, st_ss.at[e], st_rs.at[e], side(e)))
+    for e in (2, 4):
+        first = colour * STRIPE + (e // 2 - 1) * (STRIPE // 2)
+        mine = anc.at[:, pl.ds(pl.multiple_of(first, STRIPE // 2), STRIPE // 2)]
+        stripes.append(rcopy(mine, mine, st_ss.at[e], st_rs.at[e], side(e)))
+    for c in stripes:
+        c.start()
 
     load_w.wait()
     mine = NCTX * QT // NKV
@@ -278,16 +322,18 @@
             def _():
                 po_copies[e, c].start()
 
+    for d in (0,) + ZS:
+        ax[d, 2].wait_recv()
     project(0)
-    for e in XS:
-        for d in (0,) + ZS:
-            ax[d, e].wait_recv()
-        project(e)
-
-    @pl.when(z > 0)
-    def _():
-        for d in ZS:
-            spreads[d].wait_recv()
+    project(2)
+    for d in (0,) + ZS:
+        ax[d, 1].wait_recv()
+        ax[d, 3].wait_recv()
+    project(1)
+    project(3)
+
+    for c in stripes:
+        c.wait_recv()
 
     def anchor_head(g, carry):
         cols = pl.ds(pl.multiple_of(g * HD, HD), HD)
@@ -333,6 +379,13 @@
         @pl.when((z + d) % NZ != 0)
         def _():
             spreads[d].wait_send()
+
+    for c in stripes:
+        c.wait_send()
+
+    @pl.when(here == NZ)
+    def _():
+        far_stripe.wait_send()
 
     @pl.when(z == 0)
     def _():
@@ -381,6 +434,8 @@
             dma((2, NZ)), dma((2, NZ)),
             dma((NZ,)), dma((NZ,)),
             dma((NZ,)), dma,
+            dma, dma,
+            dma((5,)), dma((5,)),
             dma((NZ,)), dma((NZ,)),
             dma((NZ, NX)), dma((NZ, NX)),
             dma((NKV,)), dma((NKV,)),

time: 55.8 us -> 49.7 us (0.89)
  the two profiles are of different devices: /device:TPU:5 before, /device:TPU:1 now
where the time goes in v3:
time: 49.7 us; the launch traced here: 49.2 us
  Pallas kernels  45.7 us (92%)
  local copies, waits for them, and re-layouts  2.88 us (6%)
  between operations  0.65 us (1%)
    pallas_call x1, Pallas kernels, body(): pl.pallas_call(kernel, out_shape=(jax.ShapeDtypeStruct(ctx_query.shape, B...  45.7 us
    unnamed x4, local copies, waits for them, and re-layouts  2.88 us

profile of v3, /device:TPU:1, one launch (start us, length us, event | category | flops | bytes accessed | tf_op | source)
XLA Modules:
  0.0 49.2 jit_solution(7748957736546560911)
XLA Ops:
  0.6 45.7 %star.1 = (bf16[1,512,1024]{2,1,0:T(8,128)(2,1)}, bf16[32,256]{1,0:T(8,128)(2,1)}) custom-call(bf16[1,512,1024]{2,1,0:T(8,128)(2,1)} %cq_h.1, bf16[2,1,512,128]{3,2,1,0:T(8,128)(2,1)} %ckv_h.1, bf16[1,8,1024]{2,1,0:T(8,128)(2,1)} %nq_ref.1, bf16[2,1,8,128]{3,2,1,0:T(8,128)(2,1)} %nkv_ref.1, bf16[1024,256]{1,0:T(8,128)(2,1)} %w_h.1), custom_call_target="tpu_custom_call" | custom-call | tf_op jit(solution)/shard_map/star/pallas_call | solution.py:404
  46.3 0.0 copy-start
  46.3 2.3 %copy.9 = bf16[1,512,1024]{2,1,0:T(8,128)(2,1)} copy(bf16[1,512,1024]{2,1,0:T(8,128)(2,1)} %get-tuple-element.4) | data formatting | bytes 2097152
  48.6 0.0 copy-done
  48.6 0.6 %copy.10 = bf16[32,256]{1,0:T(8,128)(2,1)} copy(bf16[32,256]{1,0:T(8,128)(2,1)S(1)} %copy-done) | data formatting | bytes 32768
Async XLA Ops:
  46.3 2.3 %copy-start = (bf16[32,256]{1,0:T(8,128)(2,1)S(1)}, bf16[32,256]{1,0:T(8,128)(2,1)}, u32[]{:S(2)}) copy-start(bf16[32,256]{1,0:T(8,128)(2,1)} %get-tuple-element.5) | copy-start | bytes 49156

commit v4 on v3

--- a/solution.py
+++ b/solution.py
@@ -53,9 +53,9 @@
 
 
 def kernel(
-    cq_h, ckv_h, nq_ref, nkv_ref, w_h,
+    cq_h, ckv_h, nq_h, nkv_h, w_h,
     co_h, no_ref,
-    cq, kv, w, fresh, qbuf, anc, own_n, own_m, out, q_n, q_m,
+    cq, kv, w, nq_v, nkv_v, fresh, qbuf, anc, own_n, own_m, out, q_n, q_m,
     n_send, n_recv, st_send, st_recv, att, po, po_recv,
     loc, q_ss, q_rs, kv_ss, kv_rs, n_ss, n_rs, an_ss, an_rs, sc_ss, sc_rs, pass_ss, pass_rs, st_ss, st_rs,
     az_ss, az_rs, ax_ss, ax_rs, po_ss, po_rs,
@@ -80,6 +80,10 @@
     def kvdev(dy, dc):
         return (here, (y + dy) % NY * NC + (co + dc) % NC)
 
+    load_nq = pltpu.make_async_copy(nq_h, nq_v, loc.at[5])
+    load_nkv = pltpu.make_async_copy(nkv_h, nkv_v, loc.at[6])
+    load_nq.start()
+    load_nkv.start()
     barrier = pltpu.get_barrier_semaphore()
     peers = [zdev(d) for d in ZS] + [side(e) for e in (1, 3, 2, 4)] + [kvdev(*k) for k in KVS]
     for dev in peers:
@@ -90,9 +94,11 @@
     load_kv.start()
     load_cq.start()
     load_w.start()
-    nq = nq_ref[0].astype(F32)
+    load_nq.wait()
+    load_nkv.wait()
+    nq = nq_v[0].astype(F32)
     qbuf[0] = jnp.concatenate([nq[:, g * HD : (g + 1) * HD] for g in range(GROUP)], 0).astype(BF16)
-    nkv = nkv_ref[:, 0].astype(F32)
+    nkv = nkv_v[:, 0].astype(F32)
     fresh[0] = jnp.concatenate([nkv, jnp.zeros_like(nkv)], 1).astype(BF16)
     pl.semaphore_wait(barrier, len(peers))
 
@@ -195,32 +201,33 @@
     def _():
         far_stripe.start()
 
-    found = [(scores(q, kv[1, 0]), scores(q, kv[3, 0])) for q in qs]
-    totals, lses = [], []
-    for c in chunks:
-        old = q_m[rows[c], :][:, :1]
-        top = jnp.maximum(jnp.maximum(old, peak_of(found[c][0])), peak_of(found[c][1]))
-        n = (
-            q_n[rows[c], :] * jnp.exp2((old - top) * SCALE)
-            + weigh(found[c][0], top, with_ones(kv[1, 1]))
-            + weigh(found[c][1], top, with_ones(kv[3, 1]))
-        )
-        totals.append(n[:, :HD] / n[:, HD:])
-        lses.append(top * SCALE + jnp.log2(n[:, HD:]))
-    lse = jnp.concatenate(lses, 0).reshape(NZ, GROUP, QT, HD)
-    n_send[...] = jnp.concatenate(totals, 0).astype(BF16).reshape(NZ, ROWS, HD)
-    lane = lax.broadcasted_iota(jnp.int32, (NZ, QT, HD), 2)
-    stat = jnp.full((NZ, QT, HD), 0.0, F32)
-    for g in range(GROUP):
-        stat = jnp.where(lane == g, lse[:, g], stat)
-    st_send[...] = stat
-
+    lane = lax.broadcasted_iota(jnp.int32, (2, QT, HD), 2)
     n_copies = []
-    for d in FAR:
-        n_copies.append(rcopy(st_send.at[d], st_recv.at[d], n_ss.at[0, d], n_rs.at[0, d], zdev(NZ - d)))
-        n_copies.append(rcopy(n_send.at[d], n_recv.at[d], n_ss.at[1, d], n_rs.at[1, d], zdev(NZ - d)))
-    for c in n_copies:
-        c.start()
+    for pair in ((1, 2), (3, 0)):
+        found = {c: (scores(qs[c], kv[1, 0]), scores(qs[c], kv[3, 0])) for c in pair}
+        for c in pair:
+            old = q_m[rows[c], :][:, :1]
+            top = jnp.maximum(jnp.maximum(old, peak_of(found[c][0])), peak_of(found[c][1]))
+            n = (
+                q_n[rows[c], :] * jnp.exp2((old - top) * SCALE)
+                + weigh(found[c][0], top, with_ones(kv[1, 1]))
+                + weigh(found[c][1], top, with_ones(kv[3, 1]))
+            )
+            two = pl.ds(2 * c, 2)
+            n_send[two] = (n[:, :HD] / n[:, HD:]).astype(BF16).reshape(2, ROWS, HD)
+            lse = (top * SCALE + jnp.log2(n[:, HD:])).reshape(2, GROUP, QT, HD)
+            stat = lse[:, 0]
+            for g in range(1, GROUP):
+                stat = jnp.where(lane == g, lse[:, g], stat)
+            st_send[two] = stat
+        for d in sorted(2 * c + i for c in pair for i in range(2)):
+            if d:
+                args = (n_ss.at[0, d], n_rs.at[0, d], zdev(NZ - d))
+                n_copies.append(rcopy(st_send.at[d], st_recv.at[d], *args))
+                args = (n_ss.at[1, d], n_rs.at[1, d], zdev(NZ - d))
+                n_copies.append(rcopy(n_send.at[d], n_recv.at[d], *args))
+                n_copies[-2].start()
+                n_copies[-1].start()
 
     scatters = [rcopy(piece(p), piece(p), sc_ss.at[p], sc_rs, zdev(p)) for p in range(1, NZ)]
 
@@ -407,12 +414,14 @@
             jax.ShapeDtypeStruct(ctx_query.shape, BF16),
             jax.ShapeDtypeStruct((mine, cols), BF16),
         ),
-        in_specs=[any_space, any_space, vmem, vmem, any_space],
+        in_specs=[any_space] * 5,
         out_specs=(any_space, vmem),
         scratch_shapes=[
             pltpu.VMEM((BLK, GROUP * HD), BF16),
             pltpu.VMEM((NX, 2, BLK, HD), BF16),
             pltpu.VMEM((GROUP * HD, cols), BF16),
+            pltpu.VMEM(new_query.shape, BF16),
+            pltpu.VMEM(new_kv.shape, BF16),
             pltpu.VMEM((NX, 2, 16, HD), BF16),
             pltpu.VMEM((NZ, ROWS, HD), BF16),
             pltpu.VMEM((2, BLK, HD), BF16),
@@ -428,7 +437,7 @@
             pltpu.VMEM((NCTX, ROWS, HD), BF16),
             pltpu.VMEM((NKV, mine, cols), F32),
             pltpu.VMEM((NKV, mine, cols), F32),
-            dma((5,)),
+            dma((7,)),
             dma((NZ,)), dma((NZ,)),
             dma((11,)), dma((11,)),
             dma((2, NZ)), dma((2, NZ)),

time: 49.7 us -> 48.5 us (0.976)
  Pallas kernels: 45.7 us -> 44.8 us
    pallas_call x1, Pallas kernels: 45.7 us -> 44.8 us  [body(): pl.pallas_call(kernel, out_shape=(jax.ShapeDtypeStruct(ctx_query.shape, B...]
where the time goes in v4:
time: 48.5 us; the launch traced here: 48.3 us
  Pallas kernels  44.8 us (92%)
  local copies, waits for them, and re-layouts  2.88 us (6%)
  between operations  0.65 us (1%)
    pallas_call x1, Pallas kernels, body(): pl.pallas_call(kernel, out_shape=(jax.ShapeDtypeStruct(ctx_query.shape, B...  44.8 us
    unnamed x4, local copies, waits for them, and re-layouts  2.88 us

profile of v4, /device:TPU:1, one launch (start us, length us, event | category | flops | bytes accessed | tf_op | source)
XLA Modules:
  0.0 48.3 jit_solution(13671954544811298789)
XLA Ops:
  0.6 44.8 %star.1 = (bf16[1,512,1024]{2,1,0:T(8,128)(2,1)}, bf16[32,256]{1,0:T(8,128)(2,1)}) custom-call(bf16[1,512,1024]{2,1,0:T(8,128)(2,1)} %cq_h.1, bf16[2,1,512,128]{3,2,1,0:T(8,128)(2,1)} %ckv_h.1, bf16[1,8,1024]{2,1,0:T(8,128)(2,1)} %nq_h.1, bf16[2,1,8,128]{3,2,1,0:T(8,128)(2,1)} %nkv_h.1, bf16[1024,256]{1,0:T(8,128)(2,1)} %w_h.1), custom_call_target="tpu_custom_call" | custom-call | tf_op jit(solution)/shard_map/star/pallas_call | solution.py:411
  45.4 0.0 copy-start
  45.4 2.3 %copy.9 = bf16[1,512,1024]{2,1,0:T(8,128)(2,1)} copy(bf16[1,512,1024]{2,1,0:T(8,128)(2,1)} %get-tuple-element.4) | data formatting | bytes 2097152
  47.7 0.0 copy-done
  47.7 0.6 %copy.10 = bf16[32,256]{1,0:T(8,128)(2,1)} copy(bf16[32,256]{1,0:T(8,128)(2,1)S(1)} %copy-done) | data formatting | bytes 32768
Async XLA Ops:
  45.4 2.3 %copy-start = (bf16[32,256]{1,0:T(8,128)(2,1)S(1)}, bf16[32,256]{1,0:T(8,128)(2,1)}, u32[]{:S(2)}) copy-start(bf16[32,256]{1,0:T(8,128)(2,1)} %get-tuple-element.5) | copy-start | bytes 49156

commit v5 on v4

--- a/solution.py
+++ b/solution.py
@@ -54,9 +54,9 @@
 
 def kernel(
     cq_h, ckv_h, nq_h, nkv_h, w_h,
-    co_h, no_ref,
+    co_h, no_h,
     cq, kv, w, nq_v, nkv_v, fresh, qbuf, anc, own_n, own_m, out, q_n, q_m,
-    n_send, n_recv, st_send, st_recv, att, po, po_recv,
+    n_send, n_recv, st_send, st_recv, att, po, po_recv, no_v,
     loc, q_ss, q_rs, kv_ss, kv_rs, n_ss, n_rs, an_ss, an_rs, sc_ss, sc_rs, pass_ss, pass_rs, st_ss, st_rs,
     az_ss, az_rs, ax_ss, ax_rs, po_ss, po_rs,
 ):
@@ -307,37 +307,40 @@
     mine = NCTX * QT // NKV
     po_copies = {}
 
-    def project(e):
-        block = (x - e + NX) % NX
-        lhs = att[pl.ds(block * NZ, NZ)].astype(F32)
-        acc = jnp.zeros((NZ * QT, no_ref.shape[1]), F32)
+    def project(first, second):
+        blocks = [(x - e + NX) % NX for e in (first, second)]
+        lhs = [att[pl.ds(b * NZ, NZ)].astype(F32) for b in blocks]
+        acc = jnp.zeros((2 * NZ * QT, no_v.shape[1]), F32)
         for j in range(GROUP // 2):
-            pair = [lhs[:, g * QT : (g + 1) * QT].reshape(NZ * QT, HD) for g in (2 * j, 2 * j + 1)]
+            pair = [
+                jnp.concatenate([a[:, g * QT : (g + 1) * QT].reshape(NZ * QT, HD) for a in lhs], 0)
+                for g in (2 * j, 2 * j + 1)
+            ]
             acc = acc + jnp.dot(
                 jnp.concatenate(pair, 1).astype(BF16),
                 w[pl.ds(j * 2 * HD, 2 * HD), :],
                 preferred_element_type=F32,
             )
-        po[pl.ds(block * NC, NC)] = acc.reshape(NC, mine, acc.shape[1])
-        for c in range(NC):
-            dest = block * NC + c
-            po_copies[e, c] = rcopy(
-                po.at[dest], po_recv.at[head], po_ss.at[e * NC + c], po_rs.at[head], (here, dest)
-            )
-
-            @pl.when(dest != head)
-            def _():
-                po_copies[e, c].start()
+        for i, e in enumerate((first, second)):
+            rows = acc[i * NZ * QT : (i + 1) * NZ * QT]
+            po[pl.ds(blocks[i] * NC, NC)] = rows.reshape(NC, mine, acc.shape[1]).astype(BF16)
+            for c in range(NC):
+                dest = blocks[i] * NC + c
+                po_copies[e, c] = rcopy(
+                    po.at[dest], po_recv.at[head], po_ss.at[e * NC + c], po_rs.at[head], (here, dest)
+                )
+
+                @pl.when(dest != head)
+                def _():
+                    po_copies[e, c].start()
 
     for d in (0,) + ZS:
         ax[d, 2].wait_recv()
-    project(0)
-    project(2)
+    project(0, 2)
     for d in (0,) + ZS:
         ax[d, 1].wait_recv()
         ax[d, 3].wait_recv()
-    project(1)
-    project(3)
+    project(1, 3)
 
     for c in stripes:
         c.wait_recv()
@@ -358,17 +361,26 @@
             out[at, cols] = ((summed[:, :HD] * mine + n[:, :HD] * theirs) / total).astype(BF16)
         return carry
 
-    lax.fori_loop(0, GROUP, anchor_head, 0, unroll=4)
-    store_out = pltpu.make_async_copy(out, co_h.at[0], loc.at[4])
-    store_out.start()
-
-    total = po[head]
+    half = GROUP * HD // 2
+    stores = []
+
+    def anchor_half(i):
+        lax.fori_loop(i * GROUP // 2, (i + 1) * GROUP // 2, anchor_head, 0, unroll=4)
+        at = pl.ds(i * half, half)
+        stores.append(pltpu.make_async_copy(out.at[:, at], co_h.at[0, :, at], loc.at[4 + 3 * i]))
+        stores[i].start()
+
+    anchor_half(0)
+    anchor_half(1)
+    total = po[head].astype(F32)
     for dy, dc in KVS:
         source = (y + dy) % NY * NC + (co + dc) % NC
         rcopy(po.at[0], po_recv.at[source], po_ss.at[0], po_rs.at[source], (here, source)).wait_recv()
-        total = total + po_recv[source]
-    no_ref[...] = total.astype(BF16)
-
+        total = total + po_recv[source].astype(F32)
+    no_v[...] = total.astype(BF16)
+
+    store_new = pltpu.make_async_copy(no_v, no_h, loc.at[0])
+    store_new.start()
     for group in (q_copies, kv_copies, az, ax):
         for c in group.values():
             c.wait_send()
@@ -399,12 +411,13 @@
         for c in scatters:
             c.wait_send()
 
-    store_out.wait()
+    for c in stores:
+        c.wait()
+    store_new.wait()
 
 
 def body(ctx_query, ctx_kv, new_query, new_kv, out_weight):
     any_space = pl.BlockSpec(memory_space=pltpu.HBM)
-    vmem = pl.BlockSpec(memory_space=pltpu.VMEM)
     cols = out_weight.shape[1]
     mine = NCTX * QT // NKV
     dma = pltpu.SemaphoreType.DMA
@@ -415,7 +428,7 @@
             jax.ShapeDtypeStruct((mine, cols), BF16),
         ),
         in_specs=[any_space] * 5,
-        out_specs=(any_space, vmem),
+        out_specs=(any_space, any_space),
         scratch_shapes=[
             pltpu.VMEM((BLK, GROUP * HD), BF16),
             pltpu.VMEM((NX, 2, BLK, HD), BF16),
@@ -435,9 +448,10 @@
             pltpu.VMEM((NZ, QT, HD), F32),
             pltpu.VMEM((NZ, QT, HD), F32),
             pltpu.VMEM((NCTX, ROWS, HD), BF16),
-            pltpu.VMEM((NKV, mine, cols), F32),
-            pltpu.VMEM((NKV, mine, cols), F32),
-            dma((7,)),
+            pltpu.VMEM((NKV, mine, cols), BF16),
+            pltpu.VMEM((NKV, mine, cols), BF16),
+            pltpu.VMEM((mine, cols), BF16),
+            dma((8,)),
             dma((NZ,)), dma((NZ,)),
             dma((11,)), dma((11,)),
             dma((2, NZ)), dma((2, NZ)),

time: 48.5 us -> 47.8 us (0.986)
  Pallas kernels: 44.8 us -> 44.1 us
    pallas_call x1, Pallas kernels: 44.8 us -> 44.1 us  [body(): pl.pallas_call(kernel, out_shape=(jax.ShapeDtypeStruct(ctx_query.shape, B...]
where the time goes in v5:
time: 47.8 us; the launch traced here: 47.6 us
  Pallas kernels  44.1 us (92%)
  local copies, waits for them, and re-layouts  2.88 us (6%)
  between operations  0.65 us (1%)
    pallas_call x1, Pallas kernels, body(): pl.pallas_call(kernel, out_shape=(jax.ShapeDtypeStruct(ctx_query.shape, B...  44.1 us
    unnamed x4, local copies, waits for them, and re-layouts  2.88 us

profile of v5, /device:TPU:1, one launch (start us, length us, event | category | flops | bytes accessed | tf_op | source)
XLA Modules:
  0.0 47.6 jit_solution(15208252085116349054)
XLA Ops:
  0.6 44.1 %star.1 = (bf16[1,512,1024]{2,1,0:T(8,128)(2,1)}, bf16[32,256]{1,0:T(8,128)(2,1)}) custom-call(bf16[1,512,1024]{2,1,0:T(8,128)(2,1)} %cq_h.1, bf16[2,1,512,128]{3,2,1,0:T(8,128)(2,1)} %ckv_h.1, bf16[1,8,1024]{2,1,0:T(8,128)(2,1)} %nq_h.1, bf16[2,1,8,128]{3,2,1,0:T(8,128)(2,1)} %nkv_h.1, bf16[1024,256]{1,0:T(8,128)(2,1)} %w_h.1), custom_call_target="tpu_custom_call" | custom-call | tf_op jit(solution)/shard_map/star/pallas_call | solution.py:424
  44.7 0.0 copy-start
  44.7 2.3 %copy.9 = bf16[1,512,1024]{2,1,0:T(8,128)(2,1)} copy(bf16[1,512,1024]{2,1,0:T(8,128)(2,1)} %get-tuple-element.4) | data formatting | bytes 2097152
  47.0 0.0 copy-done
  47.0 0.6 %copy.10 = bf16[32,256]{1,0:T(8,128)(2,1)} copy(bf16[32,256]{1,0:T(8,128)(2,1)S(1)} %copy-done) | data formatting | bytes 32768
Async XLA Ops:
  44.7 2.3 %copy-start = (bf16[32,256]{1,0:T(8,128)(2,1)S(1)}, bf16[32,256]{1,0:T(8,128)(2,1)}, u32[]{:S(2)}) copy-start(bf16[32,256]{1,0:T(8,128)(2,1)} %get-tuple-element.5) | copy-start | bytes 49156

commit v6 on v5

--- a/solution.py
+++ b/solution.py
@@ -261,6 +261,17 @@
     az = {d: rcopy(att.at[here], att.at[here], az_ss.at[d], az_rs.at[d], zdev(d)) for d in ZS}
     for d in FAR:
         az[d].start()
+    @pl.when(z > 0)
+    def _():
+        rcopy(piece(0), piece(z), sc_ss.at[0], sc_rs, zdev(1)).wait_recv()
+
+    spreads = {d: rcopy(piece(z), piece(z), an_ss.at[d], an_rs.at[d], zdev(d)) for d in ZS}
+    for d in FAR:
+
+        @pl.when((z + d) % NZ != 0)
+        def _():
+            spreads[d].start()
+
     ax = {}
 
     def forward(d):
@@ -271,17 +282,6 @@
             ax[d, e].start()
 
     forward(0)
-
-    @pl.when(z > 0)
-    def _():
-        rcopy(piece(0), piece(z), sc_ss.at[0], sc_rs, zdev(1)).wait_recv()
-
-    spreads = {d: rcopy(piece(z), piece(z), an_ss.at[d], an_rs.at[d], zdev(d)) for d in ZS}
-    for d in FAR:
-
-        @pl.when((z + d) % NZ != 0)
-        def _():
-            spreads[d].start()
 
     for d in ZS:
         az[d].wait_recv()

time: 47.8 us -> 47.7 us (level)
  no operation moved by 1% of the time
where the time goes in v6:
time: 47.7 us; the launch traced here: 47.3 us
  Pallas kernels  43.8 us (92%)
  local copies, waits for them, and re-layouts  2.88 us (6%)
  between operations  0.65 us (1%)
    pallas_call x1, Pallas kernels, body(): pl.pallas_call(kernel, out_shape=(jax.ShapeDtypeStruct(ctx_query.shape, B...  43.8 us
    unnamed x4, local copies, waits for them, and re-layouts  2.88 us

profile of v6, /device:TPU:1, one launch (start us, length us, event | category | flops | bytes accessed | tf_op | source)
XLA Modules:
  0.0 47.3 jit_solution(17774206532043743253)
XLA Ops:
  0.6 43.8 %star.1 = (bf16[1,512,1024]{2,1,0:T(8,128)(2,1)}, bf16[32,256]{1,0:T(8,128)(2,1)}) custom-call(bf16[1,512,1024]{2,1,0:T(8,128)(2,1)} %cq_h.1, bf16[2,1,512,128]{3,2,1,0:T(8,128)(2,1)} %ckv_h.1, bf16[1,8,1024]{2,1,0:T(8,128)(2,1)} %nq_h.1, bf16[2,1,8,128]{3,2,1,0:T(8,128)(2,1)} %nkv_h.1, bf16[1024,256]{1,0:T(8,128)(2,1)} %w_h.1), custom_call_target="tpu_custom_call" | custom-call | tf_op jit(solution)/shard_map/star/pallas_call | solution.py:424
  44.5 0.0 copy-start
  44.5 2.3 %copy.9 = bf16[1,512,1024]{2,1,0:T(8,128)(2,1)} copy(bf16[1,512,1024]{2,1,0:T(8,128)(2,1)} %get-tuple-element.4) | data formatting | bytes 2097152
  46.7 0.0 copy-done
  46.7 0.6 %copy.10 = bf16[32,256]{1,0:T(8,128)(2,1)} copy(bf16[32,256]{1,0:T(8,128)(2,1)S(1)} %copy-done) | data formatting | bytes 32768
Async XLA Ops:
  44.5 2.3 %copy-start = (bf16[32,256]{1,0:T(8,128)(2,1)S(1)}, bf16[32,256]{1,0:T(8,128)(2,1)}, u32[]{:S(2)}) copy-start(bf16[32,256]{1,0:T(8,128)(2,1)} %get-tuple-element.5) | copy-start | bytes 49156
